TPU v7x, 32 devices: a whole 2x2x4 slice. The times are simulated.
32 devices in a mesh: row: 8 (over z, x), col: 4 (over y, core).
Axes of the slice: x: 2, y: 2, z: 4, core: 2. Of those that a mesh axis runs over, the one named last changes fastest.
Arguments:
- tokens: bfloat16 [192, 8192], P('col', 'row'), may hold values from -6 to 6
- out_grad: bfloat16 [192, 8192], P('col', 'row'), may hold values from -6 to 6
- gate_weight: bfloat16 [8192, 28672], P('row', 'col'), may hold values from -0.0625 to 0.0625
- up_weight: bfloat16 [8192, 28672], P('row', 'col'), may hold values from -0.0625 to 0.0625
- down_weight: bfloat16 [28672, 8192], P('col', 'row'), may hold values from -0.03125 to 0.03125
Outputs:
- input_grad: bfloat16 [192, 8192], P('col', 'row')
- gate_grad: bfloat16 [8192, 28672], P('row', 'col')
- up_grad: bfloat16 [8192, 28672], P('row', 'col')
- down_grad: bfloat16 [28672, 8192], P('col', 'row')
All inputs are finite; a program needn't handle non-finite values.
Results may differ from a plain program's by a relative error of at most 0.02.
Values may be sent and summed in bfloat16 or wider, within the bound.
A program may use at most 192 MiB of HBM per device.

v0:
```python
import jax
import jax.numpy as jnp
from jax import lax
from jax.sharding import PartitionSpec as P


def swiglu_back(gate, up_sum, hidden_delta):
    sigmoid = jax.nn.sigmoid(gate)
    activated = gate * sigmoid
    hidden = (activated * up_sum).astype(jnp.bfloat16)
    up_delta = (hidden_delta * activated).astype(jnp.bfloat16)
    gate_delta = (hidden_delta * up_sum * sigmoid * (1.0 + gate * (1.0 - sigmoid))).astype(
        jnp.bfloat16
    )
    return (hidden, gate_delta, up_delta)


def per_device(tokens, out_grad, gate_weight, up_weight, down_weight):
    tok_panel, grad_panel = (
        lax.all_gather(tokens, "col", axis=0, tiled=True),
        lax.all_gather(out_grad, "col", axis=0, tiled=True),
    )
    hidden_width = gate_weight.shape[1]
    contract_cols = (((1,), (1,)), ((), ()))
    contract_rows = (((0,), (0,)), ((), ()))
    gate_part = jnp.dot(tok_panel, gate_weight, preferred_element_type=jnp.float32)
    up_part = jnp.dot(tok_panel, up_weight, preferred_element_type=jnp.float32)
    delta_part = lax.dot_general(
        grad_panel, down_weight, contract_cols, preferred_element_type=jnp.float32
    )
    summed = lax.psum_scatter(
        jnp.concatenate([gate_part, up_part, delta_part], axis=1).astype(jnp.bfloat16),
        "row",
        scatter_dimension=0,
        tiled=True,
    ).astype(jnp.float32)
    share_hidden, share_gate, share_up = swiglu_back(
        summed[:, :hidden_width],
        summed[:, hidden_width : 2 * hidden_width],
        summed[:, 2 * hidden_width :],
    )
    hidden, gate_delta, up_delta = (
        lax.all_gather(share_hidden, "row", axis=0, tiled=True),
        lax.all_gather(share_gate, "row", axis=0, tiled=True),
        lax.all_gather(share_up, "row", axis=0, tiled=True),
    )
    gate_grad = lax.dot_general(
        tok_panel, gate_delta, contract_rows, preferred_element_type=jnp.float32
    ).astype(jnp.bfloat16)
    up_grad = lax.dot_general(
        tok_panel, up_delta, contract_rows, preferred_element_type=jnp.float32
    ).astype(jnp.bfloat16)
    down_grad = lax.dot_general(
        hidden, grad_panel, contract_rows, preferred_element_type=jnp.float32
    ).astype(jnp.bfloat16)
    total = lax.dot_general(
        gate_delta, gate_weight, contract_cols, preferred_element_type=jnp.float32
    )
    input_grad = lax.psum_scatter(
        (
            total
            + lax.dot_general(
                up_delta, up_weight, contract_cols, preferred_element_type=jnp.float32
            )
        ).astype(jnp.bfloat16),
        "col",
        scatter_dimension=0,
        tiled=True,
    )
    return (input_grad, gate_grad, up_grad, down_grad)


def solution(mesh):
    return jax.shard_map(
        per_device,
        mesh=mesh,
        in_specs=(
            P("col", "row"),
            P("col", "row"),
            P("row", "col"),
            P("row", "col"),
            P("col", "row"),
        ),
        out_specs=(P("col", "row"), P("row", "col"), P("row", "col"), P("col", "row")),
        check_vma=False,
    )
```

profile of v0, /device:TPU:0, one launch (start us, length us, event | category | flops | bytes accessed | tf_op | source)
XLA Modules:
  0.0 402.4 jit_solution(1023301052161668729)
XLA Ops:
  7.2 0.0 reduce-scatter.3.cloned.1.call-start
  7.2 8.1 %all_gather.15 = bf16[192,1024]{1,0:T(8,128)(2,1)S(1)} all-gather(bf16[48,1024]{1,0:T(8,128)(2,1)} %param.5), channel_id=1, replica_groups=mesh['row'=8,'col'=4] {'col'}, dimensions={0}, use_global_device_ids=true | all-gather | bytes 491520 | tf_op jit(solution)/shard_map/all_gather | solution.py:20
  15.4 0.0 copy-start.3
  15.4 8.3 %convolution_convert_fusion.2 = bf16[192,7168]{1,0:T(8,128)(2,1)S(1)} fusion(bf16[192,1024]{1,0:T(8,128)(2,1)S(1)} %all_gather.15, bf16[1024,7168]{1,0:T(8,128)(2,1)} %param.8), kind=kOutput, calls=%fused_computation.4 | convolution fusion | flops 2819948544 | bytes 17825792 | tf_op jit(solution)/shard_map/dot_general | solution.py:27
  23.7 1.0 copy-done.3
  24.7 0.0 copy-start.2
  24.7 4.4 %convolution_convert_fusion.3 = bf16[192,7168]{1,0:T(8,128)(2,1)} fusion(bf16[192,1024]{1,0:T(8,128)(2,1)S(1)} %all_gather.15, bf16[1024,7168]{1,0:T(8,128)(2,1)S(1)} %copy-done.3), kind=kOutput, calls=%fused_computation.5 | convolution fusion | flops 2819948544 | bytes 17825792 | tf_op jit(solution)/shard_map/dot_general | solution.py:26
  29.1 0.0 copy-done.2
  29.1 6.6 %all_gather.16 = bf16[192,1024]{1,0:T(8,128)(2,1)S(1)} all-gather(bf16[48,1024]{1,0:T(8,128)(2,1)S(1)} %copy-done.2), channel_id=1, replica_groups=mesh['row'=8,'col'=4] {'col'}, dimensions={0}, use_global_device_ids=true | all-gather | bytes 491520 | tf_op jit(solution)/shard_map/all_gather | solution.py:21
  35.7 11.7 %convolution_convert_fusion.1 = bf16[192,7168]{1,0:T(8,128)(2,1)} fusion(bf16[192,1024]{1,0:T(8,128)(2,1)S(1)} %all_gather.16, bf16[7168,1024]{1,0:T(8,128)(2,1)} %param.9), kind=kOutput, calls=%fused_computation.3 | convolution fusion | flops 2819948544 | bytes 17825792 | tf_op jit(solution)/shard_map/dot_general | solution.py:28
  47.3 6.1 %pad_maximum_fusion = bf16[192,21504]{1,0:T(8,128)(2,1)} fusion(bf16[192,7168]{1,0:T(8,128)(2,1)} %convolution_convert_fusion.1, bf16[192,7168]{1,0:T(8,128)(2,1)S(1)} %convolution_convert_fusion.2, bf16[192,7168]{1,0:T(8,128)(2,1)} %convolution_convert_fusion.3), kind=kLoop, calls=%fused_computation.6 | loop fusion | flops 24772608 | bytes 16515072 | tf_op jit(solution)/shard_map/concatenate | solution.py:32
  53.5 0.0 reduce-scatter.3.cloned.1.call-update
  53.5 0.0 all-gather.6.cloned.1.call-start
  53.6 147.9 %reduce-scatter.3.cloned.1.call-done = bf16[24,21504]{1,0:T(8,128)(2,1)} async-done(((bf16[192,21504]{1,0:T(8,128)(2,1)}), bf16[24,21504]{1,0:T(8,128)(2,1)}) %reduce-scatter.3.cloned.1.call-update) | async-done | bytes 1032208 | tf_op jit(solution)/shard_map/reduce_scatter | solution.py:31
  201.4 1.4 convert_element_type.31
  202.8 1.3 multiply_convert_fusion
  204.1 0.0 all-gather.6.cloned.1.call-update
  204.1 0.0 all-gather.4.cloned.1.call-start
  204.1 0.7 all-gather.4.cloned.1.call-update
  204.8 0.0 all-gather.8.cloned.1.call-start
  204.9 0.5 all-gather.8.cloned.1.call-update
  205.4 0.2 reduce-scatter.5.cloned.1.call-start
  205.6 53.6 %all-gather.6.cloned.1.call-done = bf16[192,7168]{1,0:T(8,128)(2,1)} async-done(((bf16[24,7168]{1,0:T(8,128)(2,1)}), bf16[192,7168]{1,0:T(8,128)(2,1)}) %all-gather.6.cloned.1.call-update) | async-done | bytes 2752528 | tf_op jit(solution)/shard_map/all_gather | solution.py:45
  259.3 9.4 %convert_bitcast_fusion = bf16[1024,7168]{0,1:T(8,128)(2,1)} fusion(bf16[192,7168]{1,0:T(8,128)(2,1)} %all-gather.6.cloned.1.call-done, bf16[192,1024]{1,0:T(8,128)(2,1)S(1)} %all_gather.15), kind=kOutput, calls=%fused_computation | convolution fusion | flops 2825912320 | bytes 17825792 | tf_op jit(solution)/shard_map/dot_general | solution.py:50
  268.7 20.0 %copy.10 = bf16[1024,7168]{1,0:T(8,128)(2,1)} copy(bf16[1024,7168]{0,1:T(8,128)(2,1)} %convert_bitcast_fusion) | data formatting | bytes 29360128
  288.6 28.1 %all-gather.4.cloned.1.call-done = bf16[192,7168]{1,0:T(8,128)(2,1)} async-done(((bf16[24,7168]{1,0:T(8,128)(2,1)}), bf16[192,7168]{1,0:T(8,128)(2,1)}) %all-gather.4.cloned.1.call-update) | async-done | bytes 2752528 | tf_op jit(solution)/shard_map/all_gather | solution.py:44
  316.7 9.4 %convert_bitcast_fusion.1 = bf16[1024,7168]{0,1:T(8,128)(2,1)} fusion(bf16[192,7168]{1,0:T(8,128)(2,1)} %all-gather.4.cloned.1.call-done, bf16[192,1024]{1,0:T(8,128)(2,1)S(1)} %all_gather.15), kind=kOutput, calls=%fused_computation.1 | convolution fusion | flops 2825912320 | bytes 17825792 | tf_op jit(solution)/shard_map/dot_general | solution.py:47
  326.1 0.0 copy-start.1
  326.1 20.1 %copy.9 = bf16[1024,7168]{1,0:T(8,128)(2,1)} copy(bf16[1024,7168]{0,1:T(8,128)(2,1)} %convert_bitcast_fusion.1) | data formatting | bytes 29360128
  346.2 0.0 copy-done.1
  346.2 0.0 copy-start
  346.2 9.2 %fusion.2 = f32[192,1024]{1,0:T(8,128)} fusion(bf16[192,7168]{1,0:T(8,128)(2,1)S(1)} %copy-done.1, bf16[1024,7168]{1,0:T(8,128)(2,1)} %param.7), kind=kOutput, calls=%fused_computation.14 | convolution fusion | flops 2818572288 | bytes 18219008 | tf_op jit(solution)/shard_map/dot_general | solution.py:56
  355.4 0.0 copy-done
  355.4 9.2 %fusion = bf16[192,1024]{1,0:T(8,128)(2,1)} fusion(f32[192,1024]{1,0:T(8,128)} %fusion.2, bf16[192,7168]{1,0:T(8,128)(2,1)S(1)} %copy-done, bf16[1024,7168]{1,0:T(8,128)(2,1)} %param.8), kind=kOutput, calls=%fused_computation.8 | convolution fusion | flops 2818965504 | bytes 18612224 | tf_op jit(solution)/shard_map/dot_general | solution.py:62
  364.6 0.0 reduce-scatter.5.cloned.1.call-update
  364.6 8.8 %all-gather.8.cloned.1.call-done = bf16[192,7168]{1,0:T(8,128)(2,1)} async-done(((bf16[24,7168]{1,0:T(8,128)(2,1)}), bf16[192,7168]{1,0:T(8,128)(2,1)}) %all-gather.8.cloned.1.call-update) | async-done | bytes 2752528 | tf_op jit(solution)/shard_map/all_gather | solution.py:43
  373.4 9.4 %convolution_convert_fusion = bf16[7168,1024]{1,0:T(8,128)(2,1)} fusion(bf16[192,7168]{1,0:T(8,128)(2,1)} %all-gather.8.cloned.1.call-done, bf16[192,1024]{1,0:T(8,128)(2,1)S(1)} %all_gather.16), kind=kOutput, calls=%fused_computation.2 | convolution fusion | flops 2825912320 | bytes 17825792 | tf_op jit(solution)/shard_map/dot_general | solution.py:53
  382.8 13.0 %reduce-scatter.5.cloned.1.call-done = bf16[48,1024]{1,0:T(8,128)(2,1)} async-done(((bf16[192,1024]{1,0:T(8,128)(2,1)}), bf16[48,1024]{1,0:T(8,128)(2,1)}) %reduce-scatter.5.cloned.1.call-update) | async-done | bytes 98320 | tf_op jit(solution)/shard_map/reduce_scatter | solution.py:59
Async XLA Ops:
  7.2 194.3 %reduce-scatter.3.cloned.1.call-start = ((), (), s32[]{:S(2)}) async-start(), calls=%async_computation.2 | async-start | bytes 9289728 | tf_op jit(solution)/shard_map/reduce_scatter | solution.py:31
  15.4 9.3 %copy-start.3 = (bf16[1024,7168]{1,0:T(8,128)(2,1)S(1)}, bf16[1024,7168]{1,0:T(8,128)(2,1)}, u32[]{:S(2)}) copy-start(bf16[1024,7168]{1,0:T(8,128)(2,1)} %param.7) | copy-start | bytes 44040196
  24.7 4.4 %copy-start.2 = (bf16[48,1024]{1,0:T(8,128)(2,1)S(1)}, bf16[48,1024]{1,0:T(8,128)(2,1)}, u32[]{:S(2)}) copy-start(bf16[48,1024]{1,0:T(8,128)(2,1)} %param.6) | copy-start | bytes 294916
  53.5 205.7 %all-gather.6.cloned.1.call-start = ((), (), s32[]{:S(2)}) async-start(), calls=%async_computation.4 | async-start | bytes 3096576 | tf_op jit(solution)/shard_map/all_gather | solution.py:45
  204.1 112.6 %all-gather.4.cloned.1.call-start = ((), (), s32[]{:S(2)}) async-start(), calls=%async_computation.3 | async-start | bytes 3096576 | tf_op jit(solution)/shard_map/all_gather | solution.py:44
  204.8 168.6 %all-gather.8.cloned.1.call-start = ((), (), s32[]{:S(2)}) async-start(), calls=%async_computation.6 | async-start | bytes 3096576 | tf_op jit(solution)/shard_map/all_gather | solution.py:43
  205.4 190.4 %reduce-scatter.5.cloned.1.call-start = ((), (), s32[]{:S(2)}) async-start(), calls=%async_computation.5 | async-start | bytes 491520 | tf_op jit(solution)/shard_map/reduce_scatter | solution.py:59
  326.1 20.1 %copy-start.1 = (bf16[192,7168]{1,0:T(8,128)(2,1)S(1)}, bf16[192,7168]{1,0:T(8,128)(2,1)}, u32[]{:S(2)}) copy-start(bf16[192,7168]{1,0:T(8,128)(2,1)} %all-gather.4.cloned.1.call-done) | copy-start | bytes 8257540
  346.2 9.2 %copy-start = (bf16[192,7168]{1,0:T(8,128)(2,1)S(1)}, bf16[192,7168]{1,0:T(8,128)(2,1)}, u32[]{:S(2)}) copy-start(bf16[192,7168]{1,0:T(8,128)(2,1)} %all-gather.6.cloned.1.call-done) | copy-start | bytes 8257540
Sparse Core Ops, SparseCore 0:
  53.6 147.7 reduce-scatter.2
  204.2 54.9 all-gather.5
  262.0 54.6 all-gather.3
  318.7 54.6 all-gather.7
  376.3 19.4 reduce-scatter.4
where the time goes:
time: 404 us; the launch traced here: 402 us
  waiting for transfers between devices  253 us (63%)
  matrix products  71 us (18%)
  local copies, waits for them, and re-layouts  41 us (10%)
  blocking collectives  14.7 us (4%)
  between operations  13.8 us (3%)
  other arithmetic  8.77 us (2%)
    reduce_scatter x1, waiting for transfers between devices, per_device(): lax.psum_scatter(jnp.concatenate([gate_part, up_part, delta_part], axis=1...  148 us
    all_gather x1, waiting for transfers between devices, per_device(): lax.all_gather(share_up, 'row', axis=0, tiled=True)  53.6 us
    unnamed x10, local copies, waits for them, and re-layouts  41 us
    all_gather x1, waiting for transfers between devices, per_device(): lax.all_gather(share_gate, 'row', axis=0, tiled=True)  28.1 us
    reduce_scatter x1, waiting for transfers between devices, per_device(): lax.psum_scatter((total + lax.dot_general(up_delta, up_weight, contract_c...  13 us
    dot_general x1, matrix products, per_device(): lax.dot_general(grad_panel, down_weight, contract_cols, preferred_element...  11.7 us
    dot_general x1, matrix products, per_device(): lax.dot_general(tok_panel, gate_delta, contract_rows, preferred_element_t...  9.4 us
    dot_general x1, matrix products, per_device(): lax.dot_general(hidden, grad_panel, contract_rows, preferred_element_type...  9.4 us
  transfers between devices with their start and end apart: 5, of which 5 were waited for; matrix products, arithmetic and copies ran while one was open for 22% of the time, Pallas kernels for 0%

commit v1 on v0

v1 whole, which is shorter than its diff:
```python
import functools

import jax
import jax.numpy as jnp
from jax import lax
from jax.experimental import pallas as pl
from jax.experimental.pallas import tpu as pltpu
from jax.sharding import PartitionSpec as P

OUTER = 4
CHUNKS = 7
F32, BF16 = jnp.float32, jnp.bfloat16
CONTRACT_COLS = (((1,), (1,)), ((), ()))
CONTRACT_ROWS = (((0,), (0,)), ((), ()))


def swiglu_back(gate, up_sum, hidden_delta):
    sigmoid = jax.nn.sigmoid(gate)
    activated = gate * sigmoid
    hidden = (activated * up_sum).astype(BF16)
    up_delta = (hidden_delta * activated).astype(BF16)
    gate_delta = (hidden_delta * up_sum * sigmoid * (1.0 + gate * (1.0 - sigmoid))).astype(BF16)
    return (hidden, gate_delta, up_delta)


def exchange(
    n_row, tok, grad, gate_w, up_w, down_w, out, in_grad,
    part, from_in, line, from_out, gate_buf, up_buf, down_buf, gate_two, up_two, acc,
    load_sem, two_sem, in_send, in_recv, out_send, out_recv, back_send, back_recv, wide_send, wide_recv,
):
    inner = n_row // OUTER
    total = tok.shape[0]
    rows = total // inner
    high = rows // 2
    half = out.shape[3]
    cols = half // CHUNKS
    me = lax.axis_index("row")
    mo, mi = me // inner, me % inner

    def row_of(o, i):
        return {"row": o * inner + i}

    def peer_in(s):
        return lax.rem(mi + s, inner)

    def peer_out(s):
        return lax.rem(mo + s, OUTER)

    def band(i):
        return pl.ds(pl.multiple_of(i * rows, rows), rows)

    def span(c):
        return pl.ds(pl.multiple_of(c * cols, cols), cols)

    def loads(c):
        slot = lax.rem(c, 2)
        made = []
        for h in range(2):
            at = pl.ds(pl.multiple_of(h * half + c * cols, cols), cols)
            for n, (src, dst) in enumerate(
                [
                    (gate_w.at[:, at], gate_buf.at[slot, h]),
                    (up_w.at[:, at], up_buf.at[slot, h]),
                    (down_w.at[at, :], down_buf.at[slot, h]),
                ]
            ):
                made.append(pltpu.make_async_copy(src, dst, load_sem.at[slot, 3 * h + n]))
        return made

    def loads_two(c):
        made = []
        for h in range(2):
            at = pl.ds(pl.multiple_of(h * half + c * cols, cols), cols)
            made.append(pltpu.make_async_copy(gate_w.at[:, at], gate_two.at[h], two_sem.at[h]))
            made.append(pltpu.make_async_copy(up_w.at[:, at], up_two.at[h], two_sem.at[2 + h]))
        return made

    def send_in(c, s):
        return pltpu.make_async_remote_copy(
            part.at[c, :, :, band(peer_in(s))], from_in.at[s - 1, c],
            in_send.at[s - 1, c], in_recv.at[s - 1, c], device_id=row_of(mo, peer_in(s)),
        )

    def send_out(c, s):
        o = peer_out(s)
        src = line.at[c, :, o % 2, pl.ds(pl.multiple_of(o // 2 * high, high), high)]
        return pltpu.make_async_remote_copy(
            src, from_out.at[s - 1, c],
            out_send.at[s - 1, c], out_recv.at[s - 1, c], device_id=row_of(o, mi),
        )

    my_rows = pl.ds(pl.multiple_of(mi * rows + mo // 2 * high, high), high)

    def send_back(c, s):
        here = out.at[:, mo % 2, my_rows, span(c)]
        return pltpu.make_async_remote_copy(
            here, here, back_send.at[s - 1, c], back_recv.at[s - 1, c],
            device_id=row_of(peer_out(s), mi),
        )

    def send_wide(c, s):
        here = out.at[:, :, band(mi), span(c)]
        return pltpu.make_async_remote_copy(
            here, here, wide_send.at[s - 1, c], wide_recv.at[s - 1, c],
            device_id=row_of(mo, peer_in(s)),
        )

    for copy in loads(0):
        copy.start()
    barrier = pltpu.get_barrier_semaphore()
    for s in range(1, inner):
        pl.semaphore_signal(barrier, inc=1, device_id=row_of(mo, peer_in(s)))
    for s in range(1, OUTER):
        pl.semaphore_signal(barrier, inc=1, device_id=row_of(peer_out(s), mi))
    pl.semaphore_wait(barrier, inner - 1 + OUTER - 1)

    acc[...] = jnp.zeros_like(acc)

    def step(t, carry):
        @pl.when(t >= 4)
        def _():
            for copy in loads_two(t - 4):
                copy.start()

        @pl.when(t < CHUNKS)
        def _():
            c = t
            slot = lax.rem(c, 2)

            @pl.when(c + 1 < CHUNKS)
            def _():
                for copy in loads(c + 1):
                    copy.start()

            for copy in loads(c):
                copy.wait()
            for h in range(2):
                part[c, 0, h] = jnp.dot(
                    tok[...], gate_buf[slot, h], preferred_element_type=F32
                ).astype(BF16)
                part[c, 1, h] = jnp.dot(
                    tok[...], up_buf[slot, h], preferred_element_type=F32
                ).astype(BF16)
                part[c, 2, h] = lax.dot_general(
                    grad[...], down_buf[slot, h], CONTRACT_COLS, preferred_element_type=F32
                ).astype(BF16)
            for s in range(1, inner):
                send_in(c, s).start()

        @pl.when((t >= 1) & (t < CHUNKS + 1))
        def _():
            c = t - 1
            for s in range(1, inner):
                send_in(c, s).wait_recv()
            for k in range(3):
                for h in range(2):
                    value = part[c, k, h, band(mi)].astype(F32)
                    for s in range(1, inner):
                        value = value + from_in[s - 1, c, k, h].astype(F32)
                    line[c, k, h] = value.astype(BF16)
            for s in range(1, OUTER):
                send_out(c, s).start()

        @pl.when((t >= 2) & (t < CHUNKS + 2))
        def _():
            c = t - 2
            for s in range(1, OUTER):
                send_out(c, s).wait_recv()
            sums = []
            for k in range(3):
                value = line[
                    c, k, mo % 2, pl.ds(pl.multiple_of(mo // 2 * high, high), high)
                ].astype(F32)
                for s in range(1, OUTER):
                    value = value + from_out[s - 1, c, k].astype(F32)
                sums.append(value)
            for k, value in enumerate(swiglu_back(*sums)):
                out[k, mo % 2, my_rows, span(c)] = value
            for s in range(1, OUTER):
                send_back(c, s).start()

        @pl.when((t >= 3) & (t < CHUNKS + 3))
        def _():
            c = t - 3
            for s in range(1, OUTER):
                send_back(c, s).wait_recv()
            for s in range(1, inner):
                send_wide(c, s).start()

        @pl.when(t >= 4)
        def _():
            c = t - 4
            for s in range(1, inner):
                send_wide(c, s).wait_recv()
            for copy in loads_two(c):
                copy.wait()
            for h in range(2):
                acc[...] += lax.dot_general(
                    out[1, h, :, span(c)], gate_two[h], CONTRACT_COLS, preferred_element_type=F32
                ) + lax.dot_general(
                    out[2, h, :, span(c)], up_two[h], CONTRACT_COLS, preferred_element_type=F32
                )

        return carry

    lax.fori_loop(0, CHUNKS + 4, step, 0)
    in_grad[...] = acc[...].astype(BF16)

    def finish(c, carry):
        for s in range(1, inner):
            send_in(c, s).wait_send()
            send_wide(c, s).wait_send()
        for s in range(1, OUTER):
            send_out(c, s).wait_send()
            send_back(c, s).wait_send()
        return carry

    lax.fori_loop(0, CHUNKS, finish, 0)


def grads(tok_t, grad, hidden, gate_delta, up_delta, gate_out, up_out, down_out):
    gate_out[...] = jnp.dot(tok_t[...], gate_delta[0, 0], preferred_element_type=F32).astype(BF16)
    up_out[...] = jnp.dot(tok_t[...], up_delta[0, 0], preferred_element_type=F32).astype(BF16)
    down_out[...] = lax.dot_general(
        hidden[0, 0], grad[...], CONTRACT_ROWS, preferred_element_type=F32
    ).astype(BF16)


def per_device(n_row, tokens, out_grad, gate_weight, up_weight, down_weight):
    inner = n_row // OUTER
    both = lax.all_gather(jnp.stack([tokens, out_grad]), "col", axis=1, tiled=True)
    tok, grad = both[0], both[1]
    total, depth = tok.shape
    width = gate_weight.shape[1]
    half = width // 2
    cols = half // CHUNKS
    rows = total // inner
    dma = pltpu.SemaphoreType.DMA
    vmem = pl.BlockSpec(memory_space=pltpu.VMEM)
    anywhere = pl.BlockSpec(memory_space=pl.ANY)
    every, in_part = pl.pallas_call(
        functools.partial(exchange, n_row),
        out_shape=(
            jax.ShapeDtypeStruct((3, 2, total, half), BF16),
            jax.ShapeDtypeStruct((total, depth), BF16),
        ),
        in_specs=[vmem, vmem, anywhere, anywhere, anywhere],
        out_specs=(vmem, vmem),
        scratch_shapes=[
            pltpu.VMEM((CHUNKS, 3, 2, total, cols), BF16),
            pltpu.VMEM((inner - 1, CHUNKS, 3, 2, rows, cols), BF16),
            pltpu.VMEM((CHUNKS, 3, 2, rows, cols), BF16),
            pltpu.VMEM((OUTER - 1, CHUNKS, 3, rows // 2, cols), BF16),
            pltpu.VMEM((2, 2, depth, cols), BF16),
            pltpu.VMEM((2, 2, depth, cols), BF16),
            pltpu.VMEM((2, 2, cols, depth), BF16),
            pltpu.VMEM((2, depth, cols), BF16),
            pltpu.VMEM((2, depth, cols), BF16),
            pltpu.VMEM((total, depth), F32),
            dma((2, 6)),
            dma((4,)),
            dma((inner - 1, CHUNKS)),
            dma((inner - 1, CHUNKS)),
            dma((OUTER - 1, CHUNKS)),
            dma((OUTER - 1, CHUNKS)),
            dma((OUTER - 1, CHUNKS)),
            dma((OUTER - 1, CHUNKS)),
            dma((inner - 1, CHUNKS)),
            dma((inner - 1, CHUNKS)),
        ],
        compiler_params=pltpu.CompilerParams(
            collective_id=0, has_side_effects=True, vmem_limit_bytes=52 * 2**20
        ),
        cost_estimate=pl.CostEstimate(
            flops=10 * total * depth * width, bytes_accessed=10 * depth * width, transcendentals=0
        ),
    )(tok, grad, gate_weight, up_weight, down_weight)
    input_grad = lax.psum_scatter(in_part, "col", scatter_dimension=0, tiled=True)

    def columns(k):
        return pl.BlockSpec((1, 1, total, cols), lambda n: (k, n // CHUNKS, 0, n % CHUNKS))

    gate_grad, up_grad, down_grad = pl.pallas_call(
        grads,
        grid=(2 * CHUNKS,),
        out_shape=(
            jax.ShapeDtypeStruct((depth, width), BF16),
            jax.ShapeDtypeStruct((depth, width), BF16),
            jax.ShapeDtypeStruct((width, depth), BF16),
        ),
        in_specs=[
            pl.BlockSpec((depth, total), lambda n: (0, 0)),
            pl.BlockSpec((total, depth), lambda n: (0, 0)),
            columns(0),
            columns(1),
            columns(2),
        ],
        out_specs=(
            pl.BlockSpec((depth, cols), lambda n: (0, n)),
            pl.BlockSpec((depth, cols), lambda n: (0, n)),
            pl.BlockSpec((cols, depth), lambda n: (n, 0)),
        ),
        compiler_params=pltpu.CompilerParams(vmem_limit_bytes=40 * 2**20),
        cost_estimate=pl.CostEstimate(
            flops=6 * total * depth * width, bytes_accessed=6 * depth * width, transcendentals=0
        ),
    )(tok.T, grad, every, every, every)
    return (input_grad, gate_grad, up_grad, down_grad)


def solution(mesh):
    return jax.shard_map(
        functools.partial(per_device, mesh.shape["row"]),
        mesh=mesh,
        in_specs=(
            P("col", "row"),
            P("col", "row"),
            P("row", "col"),
            P("row", "col"),
            P("col", "row"),
        ),
        out_specs=(P("col", "row"), P("row", "col"), P("row", "col"), P("col", "row")),
        check_vma=False,
    )
```

time: 404 us -> 271 us (0.67)
  waiting for transfers between devices: 253 us -> 7.52 us
  Pallas kernels: 0 us -> 234 us
  matrix products: 71 us -> 0 us
  local copies, waits for them, and re-layouts: 41 us -> 3.67 us
  other arithmetic: 8.77 us -> 0.96 us
  blocking collectives: 14.7 us -> 10.1 us
    pallas_call x0 -> x2, Pallas kernels: none -> 234 us  [the longest x1 217 us: per_device(): pl.pallas_call(functools.partial(exchange, n_row), out_shape=(jax.ShapeDt...]
    reduce_scatter x2 -> x1, waiting for transfers between devices: 161 us -> 7.5 us  [per_device(): lax.psum_scatter(in_part, 'col', scatter_dimension=0, tiled=True)]
    all_gather x3 -> x0, waiting for transfers between devices: 90.5 us -> none  [the longest x1 53.6 us: per_device(): lax.all_gather(share_up, 'row', axis=0, tiled=True)]
    dot_general x8 -> x0, matrix products: 71 us -> none  [the longest x1 11.7 us: per_device(): lax.dot_general(grad_panel, down_weight, contract_cols, preferred_element...]
    unnamed x10 -> x2, local copies, waits for them, and re-layouts: 41 us -> 3.34 us
    concatenate x1 -> x0, other arithmetic: 6.15 us -> none  [per_device(): jnp.concatenate([gate_part, up_part, delta_part], axis=1)]
    all_gather x2 -> x1, blocking collectives: 14.7 us -> 10.1 us  [per_device(): lax.all_gather(jnp.stack([tokens, out_grad]), 'col', axis=1, tiled=True)]
  transfers between devices with their start and end apart: 5 -> 1, of which waited for: 5 -> 1; matrix products, arithmetic and copies ran while one was open for 22% -> 0% of each run, Pallas kernels for 0% -> 7%
where the time goes in v1:
time: 271 us
  Pallas kernels  234 us (86%)
  between operations  14.1 us (5%)
  blocking collectives  10.1 us (4%)
  waiting for transfers between devices  7.52 us (3%)
  local copies, waits for them, and re-layouts  3.67 us (1%)
    pallas_call x1, Pallas kernels, per_device(): pl.pallas_call(functools.partial(exchange, n_row), out_shape=(jax.ShapeDt...  217 us
    pallas_call x1, Pallas kernels, per_device(): pl.pallas_call(grads, grid=(2 * CHUNKS,), out_shape=(jax.ShapeDtypeStruct...  17.6 us
    all_gather x1, blocking collectives, per_device(): lax.all_gather(jnp.stack([tokens, out_grad]), 'col', axis=1, tiled=True)  10.1 us
    reduce_scatter x1, waiting for transfers between devices, per_device(): lax.psum_scatter(in_part, 'col', scatter_dimension=0, tiled=True)  7.5 us
  transfers between devices with their start and end apart: 1, of which 1 were waited for; matrix products, arithmetic and copies ran while one was open for 0% of the time, Pallas kernels for 7%

profile of v1, /device:TPU:0, one launch (start us, length us, event | category | flops | bytes accessed | tf_op | source)
XLA Modules:
  0.0 270.5 jit_solution(4416149873683033389)
XLA Ops:
  7.2 0.0 reduce-scatter.2.cloned.1.call-start
  7.2 1.0 pad_maximum_fusion
  8.2 10.1 %all_gather.3 = bf16[2,192,1024]{2,1,0:T(8,128)(2,1)S(1)} all-gather(bf16[2,48,1024]{2,1,0:T(8,128)(2,1)S(1)} %pad_maximum_fusion), channel_id=1, replica_groups=mesh['row'=8,'col'=4] {'col'}, dimensions={1}, use_global_device_ids=true | all-gather | bytes 983040 | tf_op jit(solution)/shard_map/all_gather | solution.py:231
  18.2 0.1 slice_bitcast_fusion.1
  18.4 216.6 %shard_map.84 = (bf16[3,2,192,3584]{3,2,1,0:T(8,128)(2,1)}, bf16[192,1024]{1,0:T(8,128)(2,1)}) custom-call(bf16[192,1024]{1,0:T(8,128)(2,1)S(1)} %get-tuple-element.16.tok, bf16[192,1024]{1,0:T(8,128)(2,1)S(1)} %get-tuple-element.15.grad, bf16[1024,7168]{1,0:T(8,128)(2,1)} %gate_w.1, bf16[1024,7168]{1,0:T(8,128)(2,1)} %up_w.1, bf16[7168,1024]{1,0:T(8,128)(2,1)} %down_w.1), custom_call_target="tpu_custom_call" | custom-call | flops 14092861440 | bytes 73400320 | tf_op jit(solution)/shard_map/pallas_call | solution.py:241
  235.0 0.0 reduce-scatter.2.cloned.1.call-update
  235.0 0.2 copy.9.tok_t
  235.2 0.0 copy-start
  235.2 3.3 %copy-done = bf16[3,2,192,3584]{3,2,1,0:T(8,128)(2,1)S(1)} copy-done((bf16[3,2,192,3584]{3,2,1,0:T(8,128)(2,1)S(1)}, bf16[3,2,192,3584]{3,2,1,0:T(8,128)(2,1)}, u32[]{:S(2)}) %copy-start) | copy-done | bytes 8257560
  238.6 17.6 %shard_map.85 = (bf16[1024,7168]{1,0:T(8,128)(2,1)}, bf16[1024,7168]{1,0:T(8,128)(2,1)}, bf16[7168,1024]{1,0:T(8,128)(2,1)}) custom-call(bf16[1024,192]{1,0:T(8,128)(2,1)S(1)} %copy.9.tok_t, bf16[192,1024]{1,0:T(8,128)(2,1)S(1)} %get-tuple-element.15.grad, bf16[3,2,192,3584]{3,2,1,0:T(8,128)(2,1)S(1)} %copy-done, bf16[3,2,192,3584]{3,2,1,0:T(8,128)(2,1)S(1)} %copy-done, ...), custom_call_target="tpu_custom_call" | custom-call | flops 8455716864 | bytes 44040192 | tf_op jit(solution)/shard_map/pallas_call | solution.py:283
  256.2 7.5 %reduce-scatter.2.cloned.1.call-done = bf16[48,1024]{1,0:T(8,128)(2,1)} async-done(((bf16[192,1024]{1,0:T(8,128)(2,1)}), bf16[48,1024]{1,0:T(8,128)(2,1)}) %reduce-scatter.2.cloned.1.call-update) | async-done | bytes 98320 | tf_op jit(solution)/shard_map/reduce_scatter | solution.py:278
Async XLA Ops:
  7.2 256.5 %reduce-scatter.2.cloned.1.call-start = ((), (), s32[]{:S(2)}) async-start(), calls=%async_computation.1 | async-start | bytes 491520 | tf_op jit(solution)/shard_map/reduce_scatter | solution.py:278
  235.2 3.3 %copy-start = (bf16[3,2,192,3584]{3,2,1,0:T(8,128)(2,1)S(1)}, bf16[3,2,192,3584]{3,2,1,0:T(8,128)(2,1)}, u32[]{:S(2)}) copy-start(bf16[3,2,192,3584]{3,2,1,0:T(8,128)(2,1)} %get-tuple-element.10.hidden.gate_delta.up_delta) | copy-start | bytes 24772612
Sparse Core Ops, SparseCore 0:
  235.1 28.4 reduce-scatter.1
